TPU v7x, 32 devices: a whole 2x2x4 slice. The times are simulated.
32 devices in a mesh: seq: 4 (over y, core), space: 8 (over z, x).
Axes of the slice: x: 2, y: 2, z: 4, core: 2. Of those that a mesh axis runs over, the one named last changes fastest.
Arguments:
- features: bfloat16 [2048, 8192], P(None, ('seq', 'space')), may hold values from -6 to 6
- targets: bfloat16 [2048, 8192], P(None, ('seq', 'space')), may hold values from -6 to 6
- write_keys: bfloat16 [128, 8192], P(None, ('seq', 'space')), may hold values from -0.5 to 0.5
- read_queries: bfloat16 [128, 8192], P(None, ('seq', 'space')), may hold values from -0.0625 to 0.0625
- decay_codes: int32 [32, 8192], P('space', 'seq'), may hold values from 0 to 99, as said below
- scan_order: int32 [2048], replicated, may hold values from 0 to 2047, each once
- masked: int32 [6144], P(('seq', 'space')), may hold values from 0 to 8191, as said below
- skip_gain: float32 [32], P('space'), may hold values from 0.5 to 1.5
Outputs:
- mixed: bfloat16 [2048, 8192], P(None, ('seq', 'space'))
- grad_features: bfloat16 [2048, 8192], P(None, ('seq', 'space'))
Inputs may be any that keep to these rules, and one draw needn't show every extreme that they name: `decay_codes`: a token's decay factor for its head is exp(-(0.065536 / 8192) code). `masked`: entries k * 192 to (k + 1) * 192 - 1 are distinct indices among tokens k * 256 to (k + 1) * 256 - 1.
All inputs are finite; a program needn't handle non-finite values.
Results may differ from a plain program's by a relative error of at most 0.0034.
Values may be sent and summed in bfloat16 or wider, within the bound.
A program may use at most 128 MiB of HBM per device.

v0:
```python
from functools import partial

import jax
import jax.numpy as jnp
from jax import lax
from jax.sharding import PartitionSpec as P

highest = lax.Precision.HIGHEST


def prefix(part, axis, combine, identity, reverse):
    count = lax.axis_size(axis)
    place = lax.axis_index(axis)
    ahead = count - 1 - place if reverse else place
    gathered = jax.tree.map(lambda a: lax.all_gather(a, axis), part)
    state = jax.tree.map(lambda a, e: jnp.zeros_like(a) + jnp.asarray(e, a.dtype), part, identity)

    def one(lap, state):
        source = count - 1 - lap if reverse else lap
        return combine(
            state, jax.tree.map(lambda a: lax.dynamic_index_in_dim(a, source, 0, False), gathered)
        )

    return lax.fori_loop(0, ahead, one, state)


def fading(amount, unit):
    return jnp.exp(-unit * amount.astype(jnp.float32))


def combine(unit, earlier, latter):
    return (earlier[0] + latter[0], earlier[1] * fading(latter[0], unit)[:, None, None] + latter[1])


def block_pass(values, into_state, from_state, running, block_size, unit):
    head_count, head_width, length = values.shape
    state_count = into_state.shape[0]
    block_count = length // block_size
    zero_state = jnp.zeros((head_count, state_count, head_width), jnp.float32)

    def pieces(block_index):
        block_start = block_index * block_size
        value_block = lax.dynamic_slice_in_dim(values, block_start, block_size, 2)
        into_block = lax.dynamic_slice_in_dim(into_state, block_start, block_size, 1)
        from_block = lax.dynamic_slice_in_dim(from_state, block_start, block_size, 1)
        step_block = lax.dynamic_slice_in_dim(running, block_start, block_size, 1)
        earlier = lax.dynamic_slice_in_dim(running, jnp.maximum(block_start - 1, 0), 1, 1)[:, 0]
        earlier = jnp.where(block_index > 0, earlier, jnp.zeros_like(earlier))
        return (value_block, into_block, from_block, step_block, earlier)

    def forward_blocks(state_sum, block_index):
        value_block, into_block, from_block, step_block, earlier = pieces(block_index)
        latest = step_block[:, -1]
        gram_block = jnp.einsum(
            "ns,nt->st", into_block, from_block, preferred_element_type=jnp.float32
        )
        spread = jnp.abs(step_block[:, None, :] - step_block[:, :, None])
        weights = (gram_block[None] * fading(spread, unit)).astype(jnp.bfloat16)
        inside = jnp.einsum(
            "hps,hst->hpt", value_block, weights, preferred_element_type=jnp.float32
        )
        readout = jnp.einsum(
            "hnp,nt->hpt", state_sum, from_block.astype(jnp.float32), precision=highest
        )
        readout = readout * fading(step_block - earlier[:, None], unit)[:, None, :]
        scaled = (
            into_block.astype(jnp.float32)[None]
            * fading(latest[:, None] - step_block, unit)[:, None, :]
        )
        update = jnp.einsum(
            "hns,hps->hnp", scaled, value_block.astype(jnp.float32), precision=highest
        )
        state_sum = state_sum * fading(latest - earlier, unit)[:, None, None] + update
        return (state_sum, inside + readout)

    def reverse_blocks(state_sum, block_index):
        value_block, into_block, from_block, step_block, earlier = pieces(block_index)
        latest = step_block[:, -1]
        readout = jnp.einsum(
            "hnp,nt->hpt", state_sum, from_block.astype(jnp.float32), precision=highest
        )
        readout = readout * fading(latest[:, None] - step_block, unit)[:, None, :]
        scaled = (
            into_block.astype(jnp.float32)[None]
            * fading(step_block - earlier[:, None], unit)[:, None, :]
        )
        update = jnp.einsum(
            "hns,hps->hnp", scaled, value_block.astype(jnp.float32), precision=highest
        )
        state_sum = state_sum * fading(latest - earlier, unit)[:, None, None] + update
        return (state_sum, readout)

    ahead_sum, forward_out = lax.scan(forward_blocks, zero_state, jnp.arange(block_count))
    behind, reverse_out = lax.scan(
        reverse_blocks, zero_state, jnp.arange(block_count), reverse=True
    )
    own_part = jnp.moveaxis(forward_out + reverse_out, 0, 2).reshape(head_count, head_width, length)
    return (own_part, ahead_sum, behind)


def pass_states(totals, ahead_sum, behind, unit):
    joiner = partial(combine, unit)
    identity_pair = (jnp.zeros_like(totals), jnp.zeros_like(ahead_sum))
    from_before = prefix((totals, ahead_sum), "seq", joiner, identity_pair, False)[1]
    from_after = prefix((totals, behind), "seq", joiner, identity_pair, True)[1]
    return (from_before, from_after)


def incoming(from_state, running, totals, from_before, from_after, unit):
    read_wide = from_state.astype(jnp.float32)
    reached = (
        jnp.einsum("hnp,nl->hpl", from_before, read_wide, precision=highest)
        * fading(running, unit)[:, None, :]
    )
    reached = (
        reached
        + jnp.einsum("hnp,nl->hpl", from_after, read_wide, precision=highest)
        * fading(totals[:, None] - running, unit)[:, None, :]
    )
    return reached


def per_device(
    features, targets, write_keys, read_queries, decay_codes, scan_order, masked, skip_gain
):
    space_size = lax.axis_size("space")
    seq_size = lax.axis_size("seq")
    head_count = decay_codes.shape[0]
    tok_dev = features.shape[1]
    unit = 0.065536 / (tok_dev * space_size * seq_size)
    head_width = features.shape[0] // (head_count * space_size)
    first_token = (lax.axis_index("seq") * space_size + lax.axis_index("space")) * tok_dev
    slot_grid = lax.broadcasted_iota(jnp.int32, (masked.shape[0], tok_dev), 1)
    mask_row = jnp.max(
        jnp.where((masked - first_token)[:, None] == slot_grid, 1.0, 0.0), axis=0
    ).astype(jnp.float32)
    head_x = lax.all_to_all(features, "space", split_axis=0, concat_axis=1, tiled=True)
    into_state, from_state = (
        lax.all_gather(write_keys, "space", axis=1, tiled=True),
        lax.all_gather(read_queries, "space", axis=1, tiled=True),
    )
    length = head_x.shape[1]
    block_size = min(512, length)
    reverse_order = (
        jnp.zeros_like(scan_order).at[scan_order].set(jnp.arange(length, dtype=jnp.int32))
    )
    into_state = jnp.take(into_state, scan_order, axis=1)
    from_state = jnp.take(from_state, scan_order, axis=1)
    running = jnp.cumsum(jnp.take(decay_codes, scan_order, axis=1), axis=1)
    totals = running[:, -1].astype(jnp.float32)

    def mixing(values, write_side, read_side):
        own_part, ahead_sum, behind = block_pass(
            values, write_side, read_side, running, block_size, unit
        )
        from_before, from_after = pass_states(totals, ahead_sum, behind, unit)
        reached = incoming(read_side, running, totals, from_before, from_after, unit)
        return own_part + reached + skip_gain[:, None, None] * values.astype(jnp.float32)

    def to_scan(head_rows):
        return jnp.take(head_rows, scan_order, axis=1).reshape(head_count, head_width, length)

    def to_positions(scan_rows):
        return jnp.take(
            scan_rows.reshape(head_count * head_width, length), reverse_order, axis=1
        ).astype(jnp.bfloat16)

    mixed_heads = to_positions(mixing(to_scan(head_x), into_state, from_state))
    mixed = lax.all_to_all(mixed_heads, "space", split_axis=1, concat_axis=0, tiled=True)
    residue = (mask_row[None] * (mixed.astype(jnp.float32) - targets.astype(jnp.float32))).astype(
        jnp.bfloat16
    )
    residue_heads = lax.all_to_all(residue, "space", split_axis=0, concat_axis=1, tiled=True)
    grads_heads = to_positions(mixing(to_scan(residue_heads), from_state, into_state))
    grad_features = lax.all_to_all(grads_heads, "space", split_axis=1, concat_axis=0, tiled=True)
    return (mixed, grad_features)


def solution(mesh):
    return jax.shard_map(
        per_device,
        mesh=mesh,
        in_specs=(
            P(None, ("seq", "space")),
            P(None, ("seq", "space")),
            P(None, ("seq", "space")),
            P(None, ("seq", "space")),
            P("space", "seq"),
            P(),
            P(("seq", "space")),
            P("space"),
        ),
        out_specs=(P(None, ("seq", "space")), P(None, ("seq", "space"))),
        check_vma=False,
    )
```

profile of v0, /device:TPU:0, one launch (start us, length us, event | category | flops | bytes accessed | tf_op | source)
XLA Modules:
  0.0 424.8 jit_solution(18343648569118694635)
XLA Ops:
  2.9 7.4 %all-to-all-start = ((bf16[8,256,256]{1,2,0:T(8,128)(2,1)}), bf16[8,256,256]{1,2,0:T(8,128)(2,1)S(1)}, u32[]{:S(2)}, u32[]{:S(2)}) async-start(bf16[8,256,256]{1,2,0:T(8,128)(2,1)} %copy.271), calls=%async_computation | async-start | bytes 2097152 | tf_op jit(solution)/shard_map/all_to_all | solution.py:137
  11.3 5.5 %gather_fusion = s32[2048,4]{1,0:T(8,128)S(1)} fusion(s32[4,2048]{0,1:T(8,128)S(1)} %copy.268, s32[2048]{0:T(1024)S(1)} %get-tuple-element.1238), kind=kCustom, calls=%fused_computation.6 | custom fusion | bytes 73728 | tf_op jit(solution)/shard_map/jit(_take)/gather | solution.py:149
  18.8 38.6 %all_gather.41 = bf16[128,2048]{0,1:T(8,128)(2,1)S(1)} all-gather(bf16[128,256]{0,1:T(8,128)(2,1)S(1)} %copy.273), channel_id=1, replica_groups=mesh['seq'=4,'space'=8] {'space'}, dimensions={1}, use_global_device_ids=true | all-gather | bytes 589824 | tf_op jit(solution)/shard_map/all_gather | solution.py:140
  57.5 31.3 %all_gather.40 = bf16[128,2048]{0,1:T(8,128)(2,1)S(1)} all-gather(bf16[128,256]{0,1:T(8,128)(2,1)S(1)} %copy.270), channel_id=1, replica_groups=mesh['seq'=4,'space'=8] {'space'}, dimensions={1}, use_global_device_ids=true | all-gather | bytes 589824 | tf_op jit(solution)/shard_map/all_gather | solution.py:139
  89.0 6.2 %gather_fusion.3 = bf16[2048,128]{1,0:T(8,128)(2,1)S(1)} fusion(bf16[128,2048]{0,1:T(8,128)(2,1)S(1)} %all_gather.41, s32[2048]{0:T(1024)S(1)} %get-tuple-element.1238), kind=kCustom, calls=%fused_computation.4.clone | custom fusion | bytes 1056768 | tf_op jit(solution)/shard_map/jit(_take)/gather | solution.py:148
  95.2 6.2 %gather_fusion.1 = bf16[2048,128]{1,0:T(8,128)(2,1)S(1)} fusion(bf16[128,2048]{0,1:T(8,128)(2,1)S(1)} %all_gather.40, s32[2048]{0:T(1024)S(1)} %get-tuple-element.1238), kind=kCustom, calls=%fused_computation.1.clone | custom fusion | bytes 1056768 | tf_op jit(solution)/shard_map/jit(_take)/gather | solution.py:147
  105.7 5.6 %all-reduce = f32[16]{0:T(128)S(1)} all-reduce(f32[16]{0:T(128)S(1)} %dynamic-update-slice), channel_id=2, replica_groups=mesh['seq'=4,'space'=8] {'seq'}, use_global_device_ids=true, to_apply=%add | all-reduce | flops 16 | bytes 128
  112.0 8.2 %scatter_custom_fusion = s32[2048]{0:T(1024)S(1)} fusion(s32[2048]{0:T(1024)} %get-tuple-element.1237, s32[2048]{0:T(1024)S(1)} %iota.21, s32[]{:T(128)} %constant.399.clone.1), kind=kCustom, calls=%fused_computation.145 | custom fusion | bytes 8704 | tf_op jit(solution)/shard_map/scatter | solution.py:145
  121.5 9.1 %gather_fusion.2 = bf16[2048,256]{1,0:T(8,128)(2,1)} fusion(bf16[256,2048]{0,1:T(8,128)(2,1)S(1)} %bitcast.205, s32[2048]{0:T(1024)S(1)} %get-tuple-element.1238), kind=kCustom, calls=%fused_computation.clone | custom fusion | bytes 2105344 | tf_op jit(solution)/shard_map/jit(_take)/gather | solution.py:161
  136.0 24.8 %while.114 = (s32[]{:T(128)}, f32[4,128,64]{1,2,0:T(8,128)S(1)}, f32[4,4,64,512]{3,2,1,0:T(8,128)}, s32[4]{0:T(128)S(1)}, s32[4,2048]{1,0:T(4,128)S(1)}, /*index...) while((s32[]{:T(128)}, f32[4,128,64]{1,2,0:T(8,128)S(1)}, ...), condition=%wide.region_3.6_spmd, body=%wide.region_2.0_spmd.sunk | while | flops 610938880 | bytes 5711789 | solution.py:93
  162.3 17.2 %while.115 = (s32[]{:T(128)}, f32[4,128,64]{1,2,0:T(8,128)S(1)}, f32[4,4,64,512]{3,2,1,0:T(8,128)}, s32[4]{0:T(128)S(1)}, s32[4,2048]{1,0:T(4,128)S(1)}, /*index...) while((s32[]{:T(128)}, f32[4,128,64]{1,2,0:T(8,128)S(1)}, ...), condition=%wide.region_5.8_spmd, body=%wide.region_4.7_spmd.sunk | while | flops 403189792 | bytes 3056573 | solution.py:94
  183.7 7.9 %all-gather.1 = f32[16,128,64]{1,2,0:T(8,128)} all-gather(f32[4,128,64]{1,2,0:T(8,128)S(1)} %get-tuple-element.833), channel_id=3, replica_groups=mesh['seq'=4,'space'=8] {'seq'}, dimensions={0}, use_global_device_ids=true | all-gather | bytes 655360 | tf_op jit(solution)/shard_map/all_gather | solution.py:15
  191.6 12.5 %all-gather.2 = f32[16,128,64]{1,2,0:T(8,128)} all-gather(f32[4,128,64]{1,2,0:T(8,128)S(1)} %get-tuple-element.835), channel_id=4, replica_groups=mesh['seq'=4,'space'=8] {'seq'}, dimensions={0}, use_global_device_ids=true | all-gather | bytes 655360 | tf_op jit(solution)/shard_map/all_gather | solution.py:15
  204.1 5.8 %while.117 = (s32[]{:T(128)}, f32[4,128,64]{2,1,0:T(8,128)S(1)}, s32[]{:T(128)}, f32[4,4]{1,0:T(4,128)}, f32[4,4,128,64]{2,3,1,0:T(8,128)}, /*index=5*/s32[]{:T(128)}, s32[]{:T(128)}, s32[]{:T(128)}, s32[]{:T(128)}) while((s32[]{:T(128)}, f32[4,128,64]{2,1,0:T(8,128)S(1)}, s32[]{:T(128)}, f32[4,4]{1,0:T(4,128)}, ...), condition=%wide.region_9.12_spmd, body=%wide.region_8.11_spmd.sunk | while | flops 65546 | bytes 917707 | solution.py:24
  218.6 9.1 %gather_fusion.4 = bf16[2048,256]{1,0:T(8,128)(2,1)} fusion(bf16[256,2048]{0,1:T(8,128)(2,1)S(1)} %copy.287, s32[2048]{0:T(1024)S(1)} %copy-done.11), kind=kCustom, calls=%fused_computation.2.clone | custom fusion | bytes 2105344 | tf_op jit(solution)/shard_map/jit(_take)/gather | solution.py:164
  233.8 24.5 %all-to-all-done.1 = bf16[256,8,256]{0,2,1:T(8,128)(2,1)S(1)} async-done(((bf16[256,8,256]{0,2,1:T(8,128)(2,1)}), bf16[256,8,256]{0,2,1:T(8,128)(2,1)S(1)}, u32[]{:S(2)}, u32[]{:S(2)}) %all-to-all-start.1) | async-done | bytes 1048608 | tf_op jit(solution)/shard_map/all_to_all | solution.py:169
  269.5 25.8 %all-to-all-done.2 = bf16[8,256,256]{1,2,0:T(8,128)(2,1)S(1)} async-done(((bf16[8,256,256]{1,2,0:T(8,128)(2,1)}), bf16[8,256,256]{1,2,0:T(8,128)(2,1)S(1)}, u32[]{:S(2)}, u32[]{:S(2)}) %all-to-all-start.2) | async-done | bytes 1048608 | tf_op jit(solution)/shard_map/all_to_all | solution.py:173
  295.3 9.0 %gather_fusion.5 = bf16[2048,256]{1,0:T(8,128)(2,1)} fusion(bf16[256,2048]{0,1:T(8,128)(2,1)S(1)} %bitcast.206, s32[2048]{0:T(1024)S(1)} %get-tuple-element.1238), kind=kCustom, calls=%fused_computation.3.clone | custom fusion | bytes 2105344 | tf_op jit(solution)/shard_map/jit(_take)/gather | solution.py:161
  309.8 24.8 %while.118 = (s32[]{:T(128)}, f32[4,128,64]{1,2,0:T(8,128)S(1)}, f32[4,4,64,512]{3,2,1,0:T(8,128)}, s32[4]{0:T(128)S(1)}, s32[4,2048]{1,0:T(4,128)S(1)}, /*index...) while((s32[]{:T(128)}, f32[4,128,64]{1,2,0:T(8,128)S(1)}, ...), condition=%wide.region_13.17_spmd, body=%wide.region_12.16_spmd.sunk | while | flops 610938880 | bytes 5711789 | solution.py:93
  336.1 17.2 %while.119 = (s32[]{:T(128)}, f32[4,128,64]{1,2,0:T(8,128)S(1)}, f32[4,4,64,512]{3,2,1,0:T(8,128)}, s32[4]{0:T(128)S(1)}, s32[4,2048]{1,0:T(4,128)S(1)}, /*index...) while((s32[]{:T(128)}, f32[4,128,64]{1,2,0:T(8,128)S(1)}, ...), condition=%wide.region_15.19_spmd, body=%wide.region_14.18_spmd.sunk | while | flops 403189792 | bytes 3056573 | solution.py:94
  357.5 6.5 %all-gather.3 = f32[16,128,64]{1,2,0:T(8,128)S(1)} all-gather(f32[4,128,64]{1,2,0:T(8,128)S(1)} %get-tuple-element.839), channel_id=5, replica_groups=mesh['seq'=4,'space'=8] {'seq'}, dimensions={0}, use_global_device_ids=true | all-gather | bytes 655360 | tf_op jit(solution)/shard_map/all_gather | solution.py:15
  368.2 8.9 %all-gather.4 = f32[16,128,64]{1,2,0:T(8,128)S(1)} all-gather(f32[4,128,64]{1,2,0:T(8,128)S(1)} %get-tuple-element.841), channel_id=6, replica_groups=mesh['seq'=4,'space'=8] {'seq'}, dimensions={0}, use_global_device_ids=true | all-gather | bytes 655360 | tf_op jit(solution)/shard_map/all_gather | solution.py:15
  386.7 7.5 %gather_fusion.6 = bf16[2048,256]{1,0:T(8,128)(2,1)S(1)} fusion(bf16[256,2048]{0,1:T(8,128)(2,1)S(1)} %copy.304, s32[2048]{0:T(1024)S(1)} %copy-done.11), kind=kCustom, calls=%fused_computation.5.clone | custom fusion | bytes 2105344 | tf_op jit(solution)/shard_map/jit(_take)/gather | solution.py:164
  394.7 28.8 %all_to_all.76 = bf16[256,8,256]{0,2,1:T(8,128)(2,1)S(1)} all-to-all(bf16[256,8,256]{0,2,1:T(8,128)(2,1)S(1)} %bitcast.219), channel_id=1, replica_groups=mesh['seq'=4,'space'=8] {'space'}, dimensions={1} | all-to-all | bytes 2097152 | tf_op jit(solution)/shard_map/all_to_all | solution.py:175
  (274 shorter events, 145.4 us)
Async XLA Ops:
  0.6 9.7 %copy-start.9 = (s32[2048]{0:T(1024)S(1)}, s32[2048]{0:T(1024)}, u32[]{:S(2)}) copy-start(s32[2048]{0:T(1024)} %param.35) | copy-start | bytes 24580
  0.6 10.3 %copy-start.14 = (s32[4,2048]{1,0:T(4,128)S(1)}, s32[4,2048]{1,0:T(4,128)}, u32[]{:S(2)}) copy-start(s32[4,2048]{1,0:T(4,128)} %param.34) | copy-start | bytes 98308
  2.9 15.8 %copy-start.12 = (bf16[128,256]{1,0:T(8,128)(2,1)S(1)}, bf16[128,256]{1,0:T(8,128)(2,1)}, u32[]{:S(2)}) copy-start(bf16[128,256]{1,0:T(8,128)(2,1)} %param.33) | copy-start | bytes 196612
  2.9 118.6 %all-to-all-start = ((bf16[8,256,256]{1,2,0:T(8,128)(2,1)}), bf16[8,256,256]{1,2,0:T(8,128)(2,1)S(1)}, u32[]{:S(2)}, u32[]{:S(2)}) async-start(bf16[8,256,256]{1,2,0:T(8,128)(2,1)} %copy.271), calls=%async_computation | async-start | bytes 2097152 | tf_op jit(solution)/shard_map/all_to_all | solution.py:137
  10.3 47.1 %copy-start.13 = (bf16[128,256]{1,0:T(8,128)(2,1)S(1)}, bf16[128,256]{1,0:T(8,128)(2,1)}, u32[]{:S(2)}) copy-start(bf16[128,256]{1,0:T(8,128)(2,1)} %param.32) | copy-start | bytes 196612
  95.2 6.2 %copy-start = (bf16[2048,128]{1,0:T(8,128)(2,1)}, bf16[2048,128]{1,0:T(8,128)(2,1)S(1)}, u32[]{:S(2)}) copy-start(bf16[2048,128]{1,0:T(8,128)(2,1)S(1)} %gather_fusion.3) | copy-start | bytes 1572868
  95.2 6.2 %copy-start.10 = (s32[2048]{0:T(1024)S(1)}, s32[2048]{0:T(1024)}, u32[]{:S(2)}) copy-start(s32[2048]{0:T(1024)} %param.35) | copy-start | bytes 24580
  101.4 2.6 copy-start.18
  179.5 2.7 copy-start.5
  209.9 3.6 copy-start.1
  209.9 3.6 copy-start.2
  209.9 3.6 copy-start.7
  209.9 3.6 copy-start.15
  217.1 1.5 copy-start.11
  227.6 6.0 %copy-start.17 = (s32[192]{0:T(256)S(1)}, s32[192]{0:T(256)}, u32[]{:S(2)}) copy-start(s32[192]{0:T(256)} %param.36) | copy-start | bytes 2308
  229.9 28.4 %all-to-all-start.1 = ((bf16[256,8,256]{0,2,1:T(8,128)(2,1)}), bf16[256,8,256]{0,2,1:T(8,128)(2,1)S(1)}, u32[]{:S(2)}, u32[]{:S(2)}) async-start(bf16[256,8,256]{0,2,1:T(8,128)(2,1)} %bitcast.54), calls=%async_computation.1 | async-start | bytes 2097152 | tf_op jit(solution)/shard_map/all_to_all | solution.py:169
  258.3 1.0 copy-start.4
  260.7 5.2 %copy-start.3 = (bf16[8,256,256]{2,1,0:T(8,128)(2,1)}, bf16[8,256,256]{2,1,0:T(8,128)(2,1)S(1)}, u32[]{:S(2)}) copy-start(bf16[8,256,256]{2,1,0:T(8,128)(2,1)S(1)} %copy.288) | copy-start | bytes 3145732
  265.9 29.4 %all-to-all-start.2 = ((bf16[8,256,256]{1,2,0:T(8,128)(2,1)}), bf16[8,256,256]{1,2,0:T(8,128)(2,1)S(1)}, u32[]{:S(2)}, u32[]{:S(2)}) async-start(bf16[8,256,256]{1,2,0:T(8,128)(2,1)} %copy.289), calls=%async_computation.2 | async-start | bytes 2097152 | tf_op jit(solution)/shard_map/all_to_all | solution.py:173
  306.6 3.1 copy-start.6
  364.0 0.8 copy-start.8
  377.2 3.1 copy-start.16
where the time goes:
time: 426 us; the launch traced here: 425 us
  blocking collectives  140 us (33%)
  local copies, waits for them, and re-layouts  102 us (24%)
  matrix products  55.4 us (13%)
  waiting for transfers between devices  50.3 us (12%)
  other arithmetic  38 us (9%)
  loops' own time  22.2 us (5%)
  starting transfers between devices  14.7 us (3%)
    all_gather x1, blocking collectives, per_device(): lax.all_gather(read_queries, 'space', axis=1, tiled=True)  38.6 us
    all_gather x4, blocking collectives, prefix(): gathered = jax.tree.map(lambda a: lax.all_gather(a, axis), part)  35.8 us
    all_gather x1, blocking collectives, per_device(): lax.all_gather(write_keys, 'space', axis=1, tiled=True)  31.3 us
    all_to_all x1, blocking collectives, per_device(): lax.all_to_all(grads_heads, 'space', split_axis=1, concat_axis=0, tiled=T...  28.8 us
    all_to_all x1, waiting for transfers between devices, per_device(): lax.all_to_all(residue, 'space', split_axis=0, concat_axis=1, tiled=True)  25.8 us
    all_to_all x1, waiting for transfers between devices, per_device(): lax.all_to_all(mixed_heads, 'space', split_axis=1, concat_axis=0, tiled=T...  24.5 us
    dot_general x8, matrix products, forward_blocks(): jnp.einsum('hps,hst->hpt', value_block, weights, preferred_element_type=j...  19.2 us
    gather x2, local copies, waits for them, and re-layouts, to_scan(): jnp.take(head_rows, scan_order, axis=1)  18.1 us
  transfers between devices with their start and end apart: 3, of which 2 were waited for; matrix products, arithmetic and copies ran while one was open for 8% of the time, Pallas kernels for 0%

commit v1 on v0

v1 whole, which is shorter than its diff:
```python
from functools import partial

import jax
import jax.numpy as jnp
from jax import lax
from jax.experimental import pallas as pl
from jax.experimental.pallas import tpu as pltpu
from jax.sharding import PartitionSpec as P

MESH = pl.DeviceIdType.MESH
F32 = jnp.float32
BF16 = jnp.bfloat16


def dot(a, b):
    return jnp.dot(a, b, preferred_element_type=F32)


def dot_nt(a, b):
    return lax.dot_general(a, b, (((1,), (1,)), ((), ())), preferred_element_type=F32)


def xor(n, me, i):
    out, m = 0, 1
    while m < n:
        x, y = (me // m) % 2, (i // m) % 2
        out = out + m * (x + y - 2 * x * y)
        m *= 2
    return out


def kernel(
    nsp, nsq, heads, unit,
    feat, targ, keys, codes, order, gain,
    mixed_o, grad_o,
    x_s, t_s, slab, xa, xb, mix_s, grad_s, pan_m, pan_n, w_t, q_t, rank_c, rank_r, codes_f, a_s, b_s,
    tot_s, tot_r, st_s, st_r, bst, ast,
    key_ss, key_rs, x_ss, x_rs, t_ss, t_rs, m_ss, m_rs, g_ss, g_rs, tot_ss, tot_rs, st_ss, st_rs,
):
    me, mine = lax.axis_index("space"), lax.axis_index("seq")
    tok = feat.shape[1]
    rows = feat.shape[0] // nsp
    state = w_t.shape[1]
    width = rows // heads

    def chunk(i):
        return pl.ds(pl.multiple_of(i * tok, tok), tok)

    def part(i):
        return pl.ds(pl.multiple_of(i * rows, rows), rows)

    def to_space(src, dst, ss, rs, c):
        return pltpu.make_async_remote_copy(
            src_ref=src, dst_ref=dst, send_sem=ss.at[c], recv_sem=rs.at[c],
            device_id={"space": xor(nsp, me, c)}, device_id_type=MESH,
        )

    def to_seq(src, dst, ss, rs, c):
        return pltpu.make_async_remote_copy(
            src_ref=src, dst_ref=dst, send_sem=ss.at[c], recv_sem=rs.at[c],
            device_id={"seq": xor(nsq, mine, c)}, device_id_type=MESH,
        )

    barrier = pltpu.get_barrier_semaphore()
    for c in range(1, nsp):
        pl.semaphore_signal(barrier, inc=1, device_id={"space": xor(nsp, me, c)}, device_id_type=MESH)
    for c in range(1, nsq):
        pl.semaphore_signal(barrier, inc=1, device_id={"seq": xor(nsq, mine, c)}, device_id_type=MESH)
    slab[me] = keys[...]
    codes_f[...] = jnp.zeros_like(codes_f)
    codes_f[0:heads, :] = codes[...].astype(F32)
    tot_s[...] = jnp.broadcast_to(jnp.sum(codes_f[...], axis=1, keepdims=True), tot_s.shape)
    pl.semaphore_wait(barrier, nsp + nsq - 2)

    def key_copy(m, c):
        place = xor(nsp, me, c)
        return pltpu.make_async_remote_copy(
            src_ref=slab.at[place], dst_ref=slab.at[place], send_sem=key_ss.at[m + c],
            recv_sem=key_rs.at[m + c], device_id={"space": xor(nsp, me, m)}, device_id_type=MESH,
        )

    key_copies = {}

    def key_step(m):
        held = range(0, nsp, 2 * m)
        for c in held:
            if c % (4 * m):
                key_copies[c].wait_recv()
        for c in held:
            key_copies[m + c] = key_copy(m, c)
            key_copies[m + c].start()

    key_step(nsp // 2)
    tot_copies = [to_seq(tot_s, tot_r.at[c], tot_ss, tot_rs, c) for c in range(1, nsq)]
    for copy in tot_copies:
        copy.start()
    x_copies = {
        c: to_space(feat.at[part(xor(nsp, me, c)), :], x_s.at[me], x_ss, x_rs, c) for c in range(1, nsp)
    }
    for c in reversed(range(1, nsp)):
        x_copies[c].start()
    x_s[me] = feat[part(me), :]

    length = nsp * tok
    places = lax.broadcasted_iota(jnp.int32, (tok, length), 1).astype(F32)

    def rank_chunk(i, carry):
        token = lax.broadcasted_iota(jnp.int32, (tok, length), 0) + i * tok
        rank = jnp.sum(jnp.where(order[...] == token, places, 0.0), axis=1, keepdims=True)
        wide = jnp.broadcast_to(rank, (tok, 128))
        rank_c[chunk(i), :] = wide
        rank_r[i] = jnp.transpose(wide)[0:8, :]
        return carry

    lax.fori_loop(0, nsp, rank_chunk, 0)

    def before(j, k):
        col = rank_c[chunk(j), :]
        return jnp.concatenate([col] * (tok // 128), axis=1) <= rank_r[k][0:1, :]

    m = nsp // 4
    key_step(m)

    for copy in tot_copies:
        copy.wait_recv()
    offset = jnp.zeros(tot_s.shape, F32)
    for c in range(1, nsq):
        offset = offset + jnp.where(xor(nsq, mine, c) < mine, tot_r[c], 0.0)

    def run_chunk(k, carry):
        def add(j, acc):
            return acc + dot(
                codes_f[:, chunk(j)].astype(BF16), jnp.where(before(j, k), 1.0, 0.0).astype(BF16)
            )

        run = lax.fori_loop(0, nsp, add, jnp.broadcast_to(offset[:, 0:1], (codes_f.shape[0], tok)))
        a_s[k] = jnp.exp(-unit * run)
        b_s[k] = jnp.exp(unit * run)
        return carry

    lax.fori_loop(0, nsp, run_chunk, 0)

    while m > 1:
        m //= 2
        key_step(m)
    for c in range(1, nsp, 2):
        key_copies[c].wait_recv()

    def flip(i, carry):
        w_t[chunk(i), :] = jnp.transpose(slab[i, 0:state, :].astype(F32)).astype(BF16)
        q_t[chunk(i), :] = jnp.transpose(slab[i, state : 2 * state, :].astype(F32)).astype(BF16)
        return carry

    lax.fori_loop(0, nsp, flip, 0)

    def spread(ref, k):
        t = ref[k]
        return jnp.concatenate(
            [jnp.broadcast_to(t[h : h + 1, :], (width, tok)) for h in range(heads)], axis=0
        )

    def take_chunk(j, sums, side):
        value = x_s[j].astype(F32)
        va, vb = (value * spread(a_s, j)).astype(BF16), (value * spread(b_s, j)).astype(BF16)
        xa[:, chunk(j)] = va
        xb[:, chunk(j)] = vb
        into = slab[j, side : side + state, :]
        return sums[0] + dot_nt(vb, into), sums[1] + dot_nt(va, into)

    none = (jnp.zeros((rows, state), F32), jnp.zeros((rows, state), F32))

    def send_states(turn, sums):
        st_s[turn, 0] = sums[0].astype(BF16)
        st_s[turn, 1] = sums[1].astype(BF16)
        copies = []
        for c in range(1, nsq):
            there = xor(nsq, mine, c)
            which = (nsq + mine - there) // nsq
            copies.append(
                to_seq(
                    st_s.at[turn, which], st_r.at[turn, c], st_ss.at[turn], st_rs.at[turn], c
                )
            )
            copies[-1].start()
        return copies

    def take_states(turn, copies):
        early, late = jnp.zeros((rows, state), F32), jnp.zeros((rows, state), F32)
        for c in range(1, nsq):
            copies[c - 1].wait_recv()
            got = st_r[turn, c].astype(F32)
            there = xor(nsq, mine, c)
            early = early + jnp.where(there < mine, got, 0.0)
            late = late + jnp.where(there > mine, got, 0.0)
        bst[...] = early.astype(BF16)
        ast[...] = late.astype(BF16)

    def mix_chunk(k, into_t, side):
        from_k = slab[k, side : side + state, :]

        def panel(j, carry):
            gram = dot(into_t[chunk(j), :], from_k)
            ahead = before(j, k)
            pan_m[chunk(j), :] = jnp.where(ahead, gram, 0.0).astype(BF16)
            pan_n[chunk(j), :] = jnp.where(ahead, 0.0, gram).astype(BF16)
            return carry

        lax.fori_loop(0, nsp, panel, 0)
        out = spread(a_s, k) * (dot(xb[...], pan_m[...]) + dot(bst[...], from_k))
        out = out + spread(b_s, k) * (dot(xa[...], pan_n[...]) + dot(ast[...], from_k))
        value = x_s[k].astype(F32)
        skip = jnp.concatenate(
            [value[h * width : (h + 1) * width, :] * gain[h] for h in range(heads)], axis=0
        )
        return (out + skip).astype(BF16)

    sums = take_chunk(me, none, 0)
    for c in range(1, nsp):
        x_copies[c].wait_recv()
    t_copies = {
        c: to_space(targ.at[part(xor(nsp, me, c)), :], t_s.at[me], t_ss, t_rs, c) for c in range(1, nsp)
    }
    for c in reversed(range(1, nsp)):
        t_copies[c].start()
    t_s[me] = targ[part(me), :]
    sums = lax.fori_loop(1, nsp, lambda c, s: take_chunk(xor(nsp, me, c), s, 0), sums)
    states = send_states(0, sums)
    take_states(0, states)

    def forward(k, carry):
        mix_s[k] = mix_chunk(k, w_t, state)
        return carry

    lax.fori_loop(0, nsp, forward, 0)

    m_copies = {
        c: to_space(mix_s.at[xor(nsp, me, c)], mixed_o.at[part(me), :], m_ss, m_rs, c)
        for c in range(1, nsp)
    }
    for c in range(1, nsp):
        t_copies[c].wait_recv()
    for c in reversed(range(1, nsp)):
        m_copies[c].start()
    mixed_o[part(me), :] = mix_s[me]

    def residue(j, sums):
        keep = slab[j, 2 * state : 2 * state + 16, :].astype(F32)[0:1, :]
        x_s[j] = (keep * (mix_s[j].astype(F32) - t_s[j].astype(F32))).astype(BF16)
        return take_chunk(j, sums, state)

    sums = lax.fori_loop(0, nsp, residue, none)
    grad_states = send_states(1, sums)
    take_states(1, grad_states)

    def grad_copy(c):
        return to_space(grad_s.at[xor(nsp, me, c)], grad_o.at[part(me), :], g_ss, g_rs, c)

    def backward(i, carry):
        c = nsp - 1 - i
        grad_s[xor(nsp, me, c)] = mix_chunk(xor(nsp, me, c), q_t, 0)

        @pl.when(c > 0)
        def _():
            grad_copy(c).start()

        return carry

    lax.fori_loop(0, nsp, backward, 0)
    grad_o[part(me), :] = grad_s[me]

    for c in range(1, nsp):
        key_copies[c].wait_send()
        x_copies[c].wait_send()
        t_copies[c].wait_send()
    for copies in (tot_copies, states, grad_states):
        for copy in copies:
            copy.wait_send()
    for c in range(1, nsp):
        m_copies[c].wait()
        grad_copy(c).wait()


def per_device(
    features, targets, write_keys, read_queries, decay_codes, scan_order, masked, skip_gain
):
    nsp, nsq = lax.axis_size("space"), lax.axis_size("seq")
    heads = decay_codes.shape[0]
    inner, tok = features.shape
    state = write_keys.shape[0]
    length = nsp * tok
    rows = inner // nsp
    unit = 0.065536 / (length * nsq)
    first_token = (lax.axis_index("seq") * nsp + lax.axis_index("space")) * tok
    slot_grid = lax.broadcasted_iota(jnp.int32, (masked.shape[0], tok), 1)
    mask_row = jnp.max(
        jnp.where((masked - first_token)[:, None] == slot_grid, 1.0, 0.0), axis=0
    ).astype(BF16)
    keys = jnp.concatenate(
        [write_keys, read_queries, jnp.broadcast_to(mask_row[None], (16, tok))], axis=0
    )
    hp = 16 * (-(-heads // 16))
    vmem = pl.BlockSpec(memory_space=pltpu.VMEM)
    dma = pltpu.SemaphoreType.DMA
    return pl.pallas_call(
        partial(kernel, nsp, nsq, heads, unit),
        out_shape=(
            jax.ShapeDtypeStruct((inner, tok), BF16), jax.ShapeDtypeStruct((inner, tok), BF16)
        ),
        in_specs=[vmem] * 5 + [pl.BlockSpec(memory_space=pltpu.SMEM)],
        out_specs=(vmem, vmem),
        scratch_shapes=[
            pltpu.VMEM((nsp, rows, tok), BF16),
            pltpu.VMEM((nsp, rows, tok), BF16),
            pltpu.VMEM((nsp, 2 * state + 16, tok), BF16),
            pltpu.VMEM((rows, length), BF16),
            pltpu.VMEM((rows, length), BF16),
            pltpu.VMEM((nsp, rows, tok), BF16),
            pltpu.VMEM((nsp, rows, tok), BF16),
            pltpu.VMEM((length, tok), BF16),
            pltpu.VMEM((length, tok), BF16),
            pltpu.VMEM((length, state), BF16),
            pltpu.VMEM((length, state), BF16),
            pltpu.VMEM((length, 128), F32),
            pltpu.VMEM((nsp, 8, tok), F32),
            pltpu.VMEM((hp, length), F32),
            pltpu.VMEM((nsp, hp, tok), F32),
            pltpu.VMEM((nsp, hp, tok), F32),
            pltpu.VMEM((hp, 128), F32),
            pltpu.VMEM((nsq, hp, 128), F32),
            pltpu.VMEM((2, 2, rows, state), BF16),
            pltpu.VMEM((2, nsq, rows, state), BF16),
            pltpu.VMEM((rows, state), BF16),
            pltpu.VMEM((rows, state), BF16),
            *[dma((nsp,)) for _ in range(10)],
            dma((nsq,)), dma((nsq,)),
            dma((2, nsq)), dma((2, nsq)),
        ],
        compiler_params=pltpu.CompilerParams(
            collective_id=0, has_side_effects=True, vmem_limit_bytes=56 * 1024 * 1024
        ),
    )(features, targets, keys, decay_codes, scan_order.reshape(1, length), skip_gain)


def solution(mesh):
    return jax.shard_map(
        per_device,
        mesh=mesh,
        in_specs=(
            P(None, ("seq", "space")),
            P(None, ("seq", "space")),
            P(None, ("seq", "space")),
            P(None, ("seq", "space")),
            P("space", "seq"),
            P(),
            P(("seq", "space")),
            P("space"),
        ),
        out_specs=(P(None, ("seq", "space")), P(None, ("seq", "space"))),
        check_vma=False,
    )
```

time: 426 us -> 129 us (0.30)
  blocking collectives: 140 us -> 0 us
  Pallas kernels: 0 us -> 121 us
  local copies, waits for them, and re-layouts: 102 us -> 4 us
  matrix products: 55.4 us -> 0 us
  waiting for transfers between devices: 50.3 us -> 0 us
  other arithmetic: 38 us -> 1.65 us
  loops' own time: 22.2 us -> 0 us
  starting transfers between devices: 14.7 us -> 0 us
    pallas_call x0 -> x1, Pallas kernels: none -> 121 us  [per_device(): pl.pallas_call(partial(kernel, nsp, nsq, heads, unit), out_shape=(jax.Sha...]
    all_gather x6 -> x0, blocking collectives: 106 us -> none  [the longest x1 38.6 us: per_device(): lax.all_gather(read_queries, 'space', axis=1, tiled=True)]
    gather x8 -> x0, local copies, waits for them, and re-layouts: 52.8 us -> none  [the longest x2 18.1 us: to_scan(): jnp.take(head_rows, scan_order, axis=1)]
    all_to_all x3 -> x0, waiting for transfers between devices: 50.3 us -> none  [the longest x1 25.8 us: per_device(): lax.all_to_all(residue, 'space', split_axis=0, concat_axis=1, tiled=True)]
    dot_general x36 -> x0, matrix products: 49.5 us -> none  [the longest x8 19.2 us: forward_blocks(): jnp.einsum('hps,hst->hpt', value_block, weights, preferred_element_type=j...]
    all_to_all x1 -> x0, blocking collectives: 28.8 us -> none  [per_device(): lax.all_to_all(grads_heads, 'space', split_axis=1, concat_axis=0, tiled=T...]
    another operation x8 -> x0, loops' own time: 22.2 us -> none  [the longest x2 10.8 us: block_pass(): lax.scan(reverse_blocks, zero_state, jnp.arange(block_count), reverse=True)]
    all_to_all x3 -> x0, starting transfers between devices: 14.7 us -> none  [the longest x1 7.38 us: per_device(): lax.all_to_all(features, 'space', split_axis=0, concat_axis=1, tiled=True)]
  transfers between devices with their start and end apart: 3 -> 0, of which waited for: 2 -> 0; matrix products, arithmetic and copies ran while one was open for 8% -> 0% of each run, Pallas kernels for 0% -> 0%
where the time goes in v1:
time: 129 us; the launch traced here: 127 us
  Pallas kernels  121 us (94%)
  local copies, waits for them, and re-layouts  4 us (3%)
  other arithmetic  1.65 us (1%)
    pallas_call x1, Pallas kernels, per_device(): pl.pallas_call(partial(kernel, nsp, nsq, heads, unit), out_shape=(jax.Sha...  121 us
    unnamed x6, local copies, waits for them, and re-layouts  4 us

profile of v1, /device:TPU:0, one launch (start us, length us, event | category | flops | bytes accessed | tf_op | source)
XLA Modules:
  0.0 127.1 jit_solution(15147543978389386845)
XLA Ops:
  0.6 0.0 copy-start.1
  0.6 0.7 copy-done.1
  1.3 0.1 select_reduce_fusion
  1.4 1.5 %pad_maximum_fusion.keys = bf16[272,256]{1,0:T(8,128)(2,1)} fusion(bf16[16,256]{1,0:T(8,128)(2,1)S(1)} %broadcast_in_dim.17, bf16[128,256]{1,0:T(8,128)(2,1)} %param.11, bf16[128,256]{1,0:T(8,128)(2,1)} %param.10), kind=kLoop, calls=%fused_computation.2 | loop fusion | flops 417792 | bytes 278528 | tf_op jit(solution)/shard_map/concatenate | solution.py:298
  3.0 120.8 %shard_map.95 = (bf16[2048,256]{1,0:T(8,128)(2,1)}, bf16[2048,256]{1,0:T(8,128)(2,1)}) custom-call(bf16[2048,256]{1,0:T(8,128)(2,1)} %feat.1, bf16[2048,256]{1,0:T(8,128)(2,1)} %targ.1, bf16[272,256]{1,0:T(8,128)(2,1)} %pad_maximum_fusion.keys, s32[4,2048]{1,0:T(4,128)} %codes.1, s32[1,2048]{1,0:T(1,128)} %bitcast.1, f32[4]{0:T(128)} %gain.1), custom_call_target="tpu_custom_call" | custom-call | tf_op jit(solution)/shard_map/pallas_call | solution.py:304
  123.7 0.0 copy-start
  123.7 2.4 %copy.12 = bf16[2048,256]{1,0:T(8,128)(2,1)} copy(bf16[2048,256]{1,0:T(8,128)(2,1)} %get-tuple-element.4) | data formatting | bytes 2097152
  126.1 0.0 copy-done
  126.1 1.0 copy.13
  (2 shorter events, 0.0 us)
Async XLA Ops:
  0.6 0.7 copy-start.1
  123.7 2.4 %copy-start = (bf16[2048,256]{1,0:T(8,128)(2,1)S(1)}, bf16[2048,256]{1,0:T(8,128)(2,1)}, u32[]{:S(2)}) copy-start(bf16[2048,256]{1,0:T(8,128)(2,1)} %get-tuple-element.5) | copy-start | bytes 3145732

commit v2 on v1

--- a/solution.py
+++ b/solution.py
@@ -97,7 +97,7 @@
     x_copies = {
         c: to_space(feat.at[part(xor(nsp, me, c)), :], x_s.at[me], x_ss, x_rs, c) for c in range(1, nsp)
     }
-    for c in reversed(range(1, nsp)):
+    for c in range(1, nsp // 2):
         x_copies[c].start()
     x_s[me] = feat[part(me), :]
 
@@ -120,6 +120,8 @@
 
     m = nsp // 4
     key_step(m)
+    for c in reversed(range(nsp // 2, nsp)):
+        x_copies[c].start()
 
     for copy in tot_copies:
         copy.wait_recv()
@@ -161,17 +163,22 @@
 
     def take_chunk(j, sums, side):
         value = x_s[j].astype(F32)
-        va, vb = (value * spread(a_s, j)).astype(BF16), (value * spread(b_s, j)).astype(BF16)
+        ta, tb = value * spread(a_s, j), value * spread(b_s, j)
+        va, vb = ta.astype(BF16), tb.astype(BF16)
         xa[:, chunk(j)] = va
         xb[:, chunk(j)] = vb
         into = slab[j, side : side + state, :]
-        return sums[0] + dot_nt(vb, into), sums[1] + dot_nt(va, into)
+        la, lb = (ta - va.astype(F32)).astype(BF16), (tb - vb.astype(F32)).astype(BF16)
+        return (
+            sums[0] + (dot_nt(vb, into) + dot_nt(lb, into)),
+            sums[1] + (dot_nt(va, into) + dot_nt(la, into)),
+        )
 
     none = (jnp.zeros((rows, state), F32), jnp.zeros((rows, state), F32))
 
     def send_states(turn, sums):
-        st_s[turn, 0] = sums[0].astype(BF16)
-        st_s[turn, 1] = sums[1].astype(BF16)
+        st_s[turn, 0] = sums[0]
+        st_s[turn, 1] = sums[1]
         copies = []
         for c in range(1, nsq):
             there = xor(nsq, mine, c)
@@ -188,12 +195,14 @@
         early, late = jnp.zeros((rows, state), F32), jnp.zeros((rows, state), F32)
         for c in range(1, nsq):
             copies[c - 1].wait_recv()
-            got = st_r[turn, c].astype(F32)
+            got = st_r[turn, c]
             there = xor(nsq, mine, c)
             early = early + jnp.where(there < mine, got, 0.0)
             late = late + jnp.where(there > mine, got, 0.0)
-        bst[...] = early.astype(BF16)
-        ast[...] = late.astype(BF16)
+        for ref, total in ((bst, early), (ast, late)):
+            high = total.astype(BF16)
+            ref[0] = high
+            ref[1] = (total - high.astype(F32)).astype(BF16)
 
     def mix_chunk(k, into_t, side):
         from_k = slab[k, side : side + state, :]
@@ -206,8 +215,8 @@
             return carry
 
         lax.fori_loop(0, nsp, panel, 0)
-        out = spread(a_s, k) * (dot(xb[...], pan_m[...]) + dot(bst[...], from_k))
-        out = out + spread(b_s, k) * (dot(xa[...], pan_n[...]) + dot(ast[...], from_k))
+        out = spread(a_s, k) * (dot(xb[...], pan_m[...]) + (dot(bst[0], from_k) + dot(bst[1], from_k)))
+        out = out + spread(b_s, k) * (dot(xa[...], pan_n[...]) + (dot(ast[0], from_k) + dot(ast[1], from_k)))
         value = x_s[k].astype(F32)
         skip = jnp.concatenate(
             [value[h * width : (h + 1) * width, :] * gain[h] for h in range(heads)], axis=0
@@ -215,32 +224,35 @@
         return (out + skip).astype(BF16)
 
     sums = take_chunk(me, none, 0)
-    for c in range(1, nsp):
-        x_copies[c].wait_recv()
     t_copies = {
         c: to_space(targ.at[part(xor(nsp, me, c)), :], t_s.at[me], t_ss, t_rs, c) for c in range(1, nsp)
     }
     for c in reversed(range(1, nsp)):
+        x_copies[c].wait_send()
         t_copies[c].start()
+    for c in range(1, nsp):
+        x_copies[c].wait_recv()
     t_s[me] = targ[part(me), :]
     sums = lax.fori_loop(1, nsp, lambda c, s: take_chunk(xor(nsp, me, c), s, 0), sums)
     states = send_states(0, sums)
     take_states(0, states)
 
-    def forward(k, carry):
-        mix_s[k] = mix_chunk(k, w_t, state)
+    def mixed_copy(c):
+        return to_space(mix_s.at[xor(nsp, me, c)], mixed_o.at[part(me), :], m_ss, m_rs, c)
+
+    def forward(i, carry):
+        c = nsp - 1 - i
+        mix_s[xor(nsp, me, c)] = mix_chunk(xor(nsp, me, c), w_t, state)
+
+        @pl.when(c > 0)
+        def _():
+            mixed_copy(c).start()
+
         return carry
 
     lax.fori_loop(0, nsp, forward, 0)
-
-    m_copies = {
-        c: to_space(mix_s.at[xor(nsp, me, c)], mixed_o.at[part(me), :], m_ss, m_rs, c)
-        for c in range(1, nsp)
-    }
     for c in range(1, nsp):
         t_copies[c].wait_recv()
-    for c in reversed(range(1, nsp)):
-        m_copies[c].start()
     mixed_o[part(me), :] = mix_s[me]
 
     def residue(j, sums):
@@ -270,13 +282,12 @@
 
     for c in range(1, nsp):
         key_copies[c].wait_send()
-        x_copies[c].wait_send()
         t_copies[c].wait_send()
     for copies in (tot_copies, states, grad_states):
         for copy in copies:
             copy.wait_send()
     for c in range(1, nsp):
-        m_copies[c].wait()
+        mixed_copy(c).wait()
         grad_copy(c).wait()
 
 
@@ -327,10 +338,10 @@
             pltpu.VMEM((nsp, hp, tok), F32),
             pltpu.VMEM((hp, 128), F32),
             pltpu.VMEM((nsq, hp, 128), F32),
-            pltpu.VMEM((2, 2, rows, state), BF16),
-            pltpu.VMEM((2, nsq, rows, state), BF16),
-            pltpu.VMEM((rows, state), BF16),
-            pltpu.VMEM((rows, state), BF16),
+            pltpu.VMEM((2, 2, rows, state), F32),
+            pltpu.VMEM((2, nsq, rows, state), F32),
+            pltpu.VMEM((2, rows, state), BF16),
+            pltpu.VMEM((2, rows, state), BF16),
             *[dma((nsp,)) for _ in range(10)],
             dma((nsq,)), dma((nsq,)),
             dma((2, nsq)), dma((2, nsq)),

time: 129 us -> 119 us (0.922); the launches traced: 127 us -> 119 us
  Pallas kernels: 121 us -> 113 us
    pallas_call x1, Pallas kernels: 121 us -> 113 us  [per_device(): pl.pallas_call(partial(kernel, nsp, nsq, heads, unit), out_shape=(jax.Sha...]
where the time goes in v2:
time: 119 us
  Pallas kernels  113 us (95%)
  local copies, waits for them, and re-layouts  4 us (3%)
  other arithmetic  1.65 us (1%)
    pallas_call x1, Pallas kernels, per_device(): pl.pallas_call(partial(kernel, nsp, nsq, heads, unit), out_shape=(jax.Sha...  113 us
    unnamed x6, local copies, waits for them, and re-layouts  4 us

profile of v2, /device:TPU:0, one launch (start us, length us, event | category | flops | bytes accessed | tf_op | source)
XLA Modules:
  0.0 119.1 jit_solution(5226541398608932243)
XLA Ops:
  0.6 0.0 copy-start.1
  0.6 0.7 copy-done.1
  1.3 0.1 select_reduce_fusion
  1.4 1.5 %pad_maximum_fusion.keys = bf16[272,256]{1,0:T(8,128)(2,1)} fusion(bf16[16,256]{1,0:T(8,128)(2,1)S(1)} %broadcast_in_dim.17, bf16[128,256]{1,0:T(8,128)(2,1)} %param.11, bf16[128,256]{1,0:T(8,128)(2,1)} %param.10), kind=kLoop, calls=%fused_computation.2 | loop fusion | flops 417792 | bytes 278528 | tf_op jit(solution)/shard_map/concatenate | solution.py:309
  3.0 112.8 %shard_map.95 = (bf16[2048,256]{1,0:T(8,128)(2,1)}, bf16[2048,256]{1,0:T(8,128)(2,1)}) custom-call(bf16[2048,256]{1,0:T(8,128)(2,1)} %feat.1, bf16[2048,256]{1,0:T(8,128)(2,1)} %targ.1, bf16[272,256]{1,0:T(8,128)(2,1)} %pad_maximum_fusion.keys, s32[4,2048]{1,0:T(4,128)} %codes.1, s32[1,2048]{1,0:T(1,128)} %bitcast.1, f32[4]{0:T(128)} %gain.1), custom_call_target="tpu_custom_call" | custom-call | tf_op jit(solution)/shard_map/pallas_call | solution.py:315
  115.8 0.0 copy-start
  115.8 2.4 %copy.12 = bf16[2048,256]{1,0:T(8,128)(2,1)} copy(bf16[2048,256]{1,0:T(8,128)(2,1)} %get-tuple-element.4) | data formatting | bytes 2097152
  118.2 0.0 copy-done
  118.2 1.0 copy.13
  (2 shorter events, 0.0 us)
Async XLA Ops:
  0.6 0.7 copy-start.1
  115.8 2.4 %copy-start = (bf16[2048,256]{1,0:T(8,128)(2,1)S(1)}, bf16[2048,256]{1,0:T(8,128)(2,1)}, u32[]{:S(2)}) copy-start(bf16[2048,256]{1,0:T(8,128)(2,1)} %get-tuple-element.5) | copy-start | bytes 3145732

commit v3 on v2

--- a/solution.py
+++ b/solution.py
@@ -31,9 +31,9 @@
 
 def kernel(
     nsp, nsq, heads, unit,
-    feat, targ, keys, codes, order, gain,
+    feat, targ, write, read, codes, order, masked, gain,
     mixed_o, grad_o,
-    x_s, t_s, slab, xa, xb, mix_s, grad_s, pan_m, pan_n, w_t, q_t, rank_c, rank_r, codes_f, a_s, b_s,
+    x_s, t_s, t_p, slab, xa, xb, mix_s, grad_s, pan_m, pan_n, w_t, q_t, rank_c, rank_r, codes_f, a_s, b_s,
     tot_s, tot_r, st_s, st_r, bst, ast,
     key_ss, key_rs, x_ss, x_rs, t_ss, t_rs, m_ss, m_rs, g_ss, g_rs, tot_ss, tot_rs, st_ss, st_rs,
 ):
@@ -66,7 +66,12 @@
         pl.semaphore_signal(barrier, inc=1, device_id={"space": xor(nsp, me, c)}, device_id_type=MESH)
     for c in range(1, nsq):
         pl.semaphore_signal(barrier, inc=1, device_id={"seq": xor(nsq, mine, c)}, device_id_type=MESH)
-    slab[me] = keys[...]
+    slab[me, 0:state, :] = write[...]
+    slab[me, state : 2 * state, :] = read[...]
+    token = lax.broadcasted_iota(jnp.int32, (tok, masked.shape[1]), 0) + (mine * nsp + me) * tok
+    hit = jnp.max(jnp.where(masked[...] == token, 1.0, 0.0), axis=1, keepdims=True)
+    hit = jnp.transpose(jnp.broadcast_to(hit, (tok, 128)))[0:16, :]
+    slab[me, 2 * state : 2 * state + 16, :] = hit.astype(BF16)
     codes_f[...] = jnp.zeros_like(codes_f)
     codes_f[0:heads, :] = codes[...].astype(F32)
     tot_s[...] = jnp.broadcast_to(jnp.sum(codes_f[...], axis=1, keepdims=True), tot_s.shape)
@@ -114,6 +119,15 @@
 
     lax.fori_loop(0, nsp, rank_chunk, 0)
 
+    def picks(j):
+        keep = slab[j, 2 * state : 2 * state + 16, :]
+        older = lax.broadcasted_iota(jnp.int32, (tok, tok), 0) <= lax.broadcasted_iota(
+            jnp.int32, (tok, tok), 1
+        )
+        count = dot(keep, jnp.where(older, 1.0, 0.0).astype(BF16))[0:1, :]
+        slot = lax.broadcasted_iota(jnp.int32, (masked.shape[1], tok), 0).astype(F32) + 1.0
+        return jnp.where(count == slot, keep.astype(F32)[0:1, :], 0.0).astype(BF16)
+
     def before(j, k):
         col = rank_c[chunk(j), :]
         return jnp.concatenate([col] * (tok // 128), axis=1) <= rank_r[k][0:1, :]
@@ -122,6 +136,12 @@
     key_step(m)
     for c in reversed(range(nsp // 2, nsp)):
         x_copies[c].start()
+
+    def pack(d, carry):
+        t_p[d] = dot_nt(picks(me), targ[part(d), :]).astype(BF16)
+        return carry
+
+    lax.fori_loop(0, nsp, pack, 0)
 
     for copy in tot_copies:
         copy.wait_recv()
@@ -225,14 +245,14 @@
 
     sums = take_chunk(me, none, 0)
     t_copies = {
-        c: to_space(targ.at[part(xor(nsp, me, c)), :], t_s.at[me], t_ss, t_rs, c) for c in range(1, nsp)
+        c: to_space(t_p.at[xor(nsp, me, c)], t_s.at[me], t_ss, t_rs, c) for c in range(1, nsp)
     }
     for c in reversed(range(1, nsp)):
         x_copies[c].wait_send()
         t_copies[c].start()
     for c in range(1, nsp):
         x_copies[c].wait_recv()
-    t_s[me] = targ[part(me), :]
+    t_s[me] = t_p[me]
     sums = lax.fori_loop(1, nsp, lambda c, s: take_chunk(xor(nsp, me, c), s, 0), sums)
     states = send_states(0, sums)
     take_states(0, states)
@@ -257,7 +277,10 @@
 
     def residue(j, sums):
         keep = slab[j, 2 * state : 2 * state + 16, :].astype(F32)[0:1, :]
-        x_s[j] = (keep * (mix_s[j].astype(F32) - t_s[j].astype(F32))).astype(BF16)
+        wanted = lax.dot_general(
+            t_s[j], picks(j), (((0,), (0,)), ((), ())), preferred_element_type=F32
+        )
+        x_s[j] = (keep * (mix_s[j].astype(F32) - wanted)).astype(BF16)
         return take_chunk(j, sums, state)
 
     sums = lax.fori_loop(0, nsp, residue, none)
@@ -301,14 +324,6 @@
     length = nsp * tok
     rows = inner // nsp
     unit = 0.065536 / (length * nsq)
-    first_token = (lax.axis_index("seq") * nsp + lax.axis_index("space")) * tok
-    slot_grid = lax.broadcasted_iota(jnp.int32, (masked.shape[0], tok), 1)
-    mask_row = jnp.max(
-        jnp.where((masked - first_token)[:, None] == slot_grid, 1.0, 0.0), axis=0
-    ).astype(BF16)
-    keys = jnp.concatenate(
-        [write_keys, read_queries, jnp.broadcast_to(mask_row[None], (16, tok))], axis=0
-    )
     hp = 16 * (-(-heads // 16))
     vmem = pl.BlockSpec(memory_space=pltpu.VMEM)
     dma = pltpu.SemaphoreType.DMA
@@ -317,11 +332,12 @@
         out_shape=(
             jax.ShapeDtypeStruct((inner, tok), BF16), jax.ShapeDtypeStruct((inner, tok), BF16)
         ),
-        in_specs=[vmem] * 5 + [pl.BlockSpec(memory_space=pltpu.SMEM)],
+        in_specs=[vmem] * 7 + [pl.BlockSpec(memory_space=pltpu.SMEM)],
         out_specs=(vmem, vmem),
         scratch_shapes=[
             pltpu.VMEM((nsp, rows, tok), BF16),
-            pltpu.VMEM((nsp, rows, tok), BF16),
+            pltpu.VMEM((nsp, masked.shape[0], rows), BF16),
+            pltpu.VMEM((nsp, masked.shape[0], rows), BF16),
             pltpu.VMEM((nsp, 2 * state + 16, tok), BF16),
             pltpu.VMEM((rows, length), BF16),
             pltpu.VMEM((rows, length), BF16),
@@ -349,7 +365,10 @@
         compiler_params=pltpu.CompilerParams(
             collective_id=0, has_side_effects=True, vmem_limit_bytes=56 * 1024 * 1024
         ),
-    )(features, targets, keys, decay_codes, scan_order.reshape(1, length), skip_gain)
+    )(
+        features, targets, write_keys, read_queries, decay_codes,
+        scan_order.reshape(1, length), masked.reshape(1, masked.shape[0]), skip_gain,
+    )
 
 
 def solution(mesh):

time: 119 us -> 116 us (0.975)
  other arithmetic: 1.65 us -> 0 us
    concatenate x1 -> x0, other arithmetic: 1.54 us -> none  [per_device(): jnp.concatenate([write_keys, read_queries, jnp.broadcast_to(mask_row[None...]
    unnamed x6 -> x4, local copies, waits for them, and re-layouts: 4 us -> 3.32 us
where the time goes in v3:
time: 116 us
  Pallas kernels  112 us (97%)
  local copies, waits for them, and re-layouts  3.32 us (3%)
    pallas_call x1, Pallas kernels, per_device(): pl.pallas_call(partial(kernel, nsp, nsq, heads, unit), out_shape=(jax.Sha...  112 us
    unnamed x4, local copies, waits for them, and re-layouts  3.32 us

profile of v3, /device:TPU:0, one launch (start us, length us, event | category | flops | bytes accessed | tf_op | source)
XLA Modules:
  0.0 116.2 jit_solution(13024667977295409522)
XLA Ops:
  0.6 112.2 %shard_map.95 = (bf16[2048,256]{1,0:T(8,128)(2,1)}, bf16[2048,256]{1,0:T(8,128)(2,1)}) custom-call(bf16[2048,256]{1,0:T(8,128)(2,1)} %feat.1, bf16[2048,256]{1,0:T(8,128)(2,1)} %targ.1, bf16[128,256]{1,0:T(8,128)(2,1)} %write.1, bf16[128,256]{1,0:T(8,128)(2,1)} %read.1, s32[4,2048]{1,0:T(4,128)} %codes.1, s32[1,2048]{1,0:T(1,128)} %bitcast.2, ...), custom_call_target="tpu_custom_call" | custom-call | tf_op jit(solution)/shard_map/pallas_call | solution.py:330
  112.9 0.0 copy-start
  112.9 2.4 %copy.12 = bf16[2048,256]{1,0:T(8,128)(2,1)} copy(bf16[2048,256]{1,0:T(8,128)(2,1)} %get-tuple-element.4) | data formatting | bytes 2097152
  115.2 0.0 copy-done
  115.2 1.0 copy.13
Async XLA Ops:
  112.9 2.4 %copy-start = (bf16[2048,256]{1,0:T(8,128)(2,1)S(1)}, bf16[2048,256]{1,0:T(8,128)(2,1)}, u32[]{:S(2)}) copy-start(bf16[2048,256]{1,0:T(8,128)(2,1)} %get-tuple-element.5) | copy-start | bytes 3145732

commit v4 on v3

--- a/solution.py
+++ b/solution.py
@@ -33,8 +33,8 @@
     nsp, nsq, heads, unit,
     feat, targ, write, read, codes, order, masked, gain,
     mixed_o, grad_o,
-    x_s, t_s, t_p, slab, xa, xb, mix_s, grad_s, pan_m, pan_n, w_t, q_t, rank_c, rank_r, codes_f, a_s, b_s,
-    tot_s, tot_r, st_s, st_r, bst, ast,
+    x_s, t_s, t_p, slab, xab, mix_s, grad_s, gm_c, gm_r, w_t, q_t, rank_c, rank_r, codes_f, a_s, b_s,
+    tot_s, tot_r, st_s, st_r, sab,
     key_ss, key_rs, x_ss, x_rs, t_ss, t_rs, m_ss, m_rs, g_ss, g_rs, tot_ss, tot_rs, st_ss, st_rs,
 ):
     me, mine = lax.axis_index("space"), lax.axis_index("seq")
@@ -181,24 +181,59 @@
             [jnp.broadcast_to(t[h : h + 1, :], (width, tok)) for h in range(heads)], axis=0
         )
 
-    def take_chunk(j, sums, side):
+    def gram(j, k):
+        tile = dot(w_t[chunk(j), :], slab[k, state : 2 * state, :])
+        return jnp.where(before(j, k), tile, 0.0).astype(BF16)
+
+    whole = gm_c.shape[1] == length
+
+    def columns(k):
+        if whole:
+            return gm_c[:, chunk(k)]
+
+        def fill(j, carry):
+            gm_c[chunk(j), :] = gram(j, k)
+            return carry
+
+        lax.fori_loop(0, nsp, fill, 0)
+        return gm_c[...]
+
+    def lines(j):
+        if whole:
+            return gm_c[chunk(j), :]
+
+        def fill(k, carry):
+            gm_r[:, chunk(k)] = gram(j, k)
+            return carry
+
+        lax.fori_loop(0, nsp, fill, 0)
+        return gm_r[...]
+
+    if whole:
+
+        def fill_all(j, carry):
+            def fill(k, carry):
+                gm_c[chunk(j), chunk(k)] = gram(j, k)
+                return carry
+
+            return lax.fori_loop(0, nsp, fill, carry)
+
+        lax.fori_loop(0, nsp, fill_all, 0)
+
+    def take_chunk(j, sums, into_t):
         value = x_s[j].astype(F32)
-        ta, tb = value * spread(a_s, j), value * spread(b_s, j)
-        va, vb = ta.astype(BF16), tb.astype(BF16)
-        xa[:, chunk(j)] = va
-        xb[:, chunk(j)] = vb
-        into = slab[j, side : side + state, :]
-        la, lb = (ta - va.astype(F32)).astype(BF16), (tb - vb.astype(F32)).astype(BF16)
-        return (
-            sums[0] + (dot_nt(vb, into) + dot_nt(lb, into)),
-            sums[1] + (dot_nt(va, into) + dot_nt(la, into)),
-        )
-
-    none = (jnp.zeros((rows, state), F32), jnp.zeros((rows, state), F32))
+        wide = jnp.concatenate([value * spread(b_s, j), value * spread(a_s, j)], axis=0)
+        high = wide.astype(BF16)
+        low = (wide - high.astype(F32)).astype(BF16)
+        xab[:, chunk(j)] = high
+        into = into_t[chunk(j), :]
+        return sums + (dot(high, into) + dot(low, into))
+
+    none = jnp.zeros((2 * rows, state), F32)
 
     def send_states(turn, sums):
-        st_s[turn, 0] = sums[0]
-        st_s[turn, 1] = sums[1]
+        st_s[turn, 0] = sums[0:rows]
+        st_s[turn, 1] = sums[rows : 2 * rows]
         copies = []
         for c in range(1, nsq):
             there = xor(nsq, mine, c)
@@ -211,58 +246,58 @@
             copies[-1].start()
         return copies
 
-    def take_states(turn, copies):
-        early, late = jnp.zeros((rows, state), F32), jnp.zeros((rows, state), F32)
+    def take_states(turn, copies, own):
+        totals = [jnp.zeros((rows, state), F32), jnp.zeros((rows, state), F32)]
+        totals[own] = st_s[turn, own]
         for c in range(1, nsq):
             copies[c - 1].wait_recv()
             got = st_r[turn, c]
             there = xor(nsq, mine, c)
-            early = early + jnp.where(there < mine, got, 0.0)
-            late = late + jnp.where(there > mine, got, 0.0)
-        for ref, total in ((bst, early), (ast, late)):
-            high = total.astype(BF16)
-            ref[0] = high
-            ref[1] = (total - high.astype(F32)).astype(BF16)
-
-    def mix_chunk(k, into_t, side):
+            totals[0] = totals[0] + jnp.where(there < mine, got, 0.0)
+            totals[1] = totals[1] + jnp.where(there > mine, got, 0.0)
+        for i in range(2):
+            high = totals[i].astype(BF16)
+            sab[i * rows : (i + 1) * rows, 0:state] = high
+            sab[i * rows : (i + 1) * rows, state : 2 * state] = (
+                totals[i] - high.astype(F32)
+            ).astype(BF16)
+
+    def finish(k, inside, side, own):
         from_k = slab[k, side : side + state, :]
-
-        def panel(j, carry):
-            gram = dot(into_t[chunk(j), :], from_k)
-            ahead = before(j, k)
-            pan_m[chunk(j), :] = jnp.where(ahead, gram, 0.0).astype(BF16)
-            pan_n[chunk(j), :] = jnp.where(ahead, 0.0, gram).astype(BF16)
-            return carry
-
-        lax.fori_loop(0, nsp, panel, 0)
-        out = spread(a_s, k) * (dot(xb[...], pan_m[...]) + (dot(bst[0], from_k) + dot(bst[1], from_k)))
-        out = out + spread(b_s, k) * (dot(xa[...], pan_n[...]) + (dot(ast[0], from_k) + dot(ast[1], from_k)))
+        far = dot(sab[...], jnp.concatenate([from_k, from_k], axis=0))
+        signs = (1.0, -1.0) if own == 1 else (-1.0, 1.0)
+        out = spread(a_s, k) * (far[0:rows] + signs[0] * inside[0:rows])
+        out = out + spread(b_s, k) * (far[rows : 2 * rows] + signs[1] * inside[rows : 2 * rows])
         value = x_s[k].astype(F32)
         skip = jnp.concatenate(
             [value[h * width : (h + 1) * width, :] * gain[h] for h in range(heads)], axis=0
         )
         return (out + skip).astype(BF16)
 
-    sums = take_chunk(me, none, 0)
+    def x_chunk(c, sums):
+        to_space(feat.at[part(xor(nsp, me, c)), :], x_s.at[me], x_ss, x_rs, c).wait_recv()
+        return take_chunk(xor(nsp, me, c), sums, w_t)
+
+    sums = take_chunk(me, none, w_t)
+    sums = lax.fori_loop(1, nsp // 2, x_chunk, sums)
     t_copies = {
         c: to_space(t_p.at[xor(nsp, me, c)], t_s.at[me], t_ss, t_rs, c) for c in range(1, nsp)
     }
     for c in reversed(range(1, nsp)):
         x_copies[c].wait_send()
         t_copies[c].start()
-    for c in range(1, nsp):
-        x_copies[c].wait_recv()
     t_s[me] = t_p[me]
-    sums = lax.fori_loop(1, nsp, lambda c, s: take_chunk(xor(nsp, me, c), s, 0), sums)
+    sums = lax.fori_loop(nsp // 2, nsp, x_chunk, sums)
     states = send_states(0, sums)
-    take_states(0, states)
+    take_states(0, states, 1)
 
     def mixed_copy(c):
         return to_space(mix_s.at[xor(nsp, me, c)], mixed_o.at[part(me), :], m_ss, m_rs, c)
 
     def forward(i, carry):
         c = nsp - 1 - i
-        mix_s[xor(nsp, me, c)] = mix_chunk(xor(nsp, me, c), w_t, state)
+        k = xor(nsp, me, c)
+        mix_s[k] = finish(k, dot(xab[...], columns(k)), state, 1)
 
         @pl.when(c > 0)
         def _():
@@ -271,8 +306,6 @@
         return carry
 
     lax.fori_loop(0, nsp, forward, 0)
-    for c in range(1, nsp):
-        t_copies[c].wait_recv()
     mixed_o[part(me), :] = mix_s[me]
 
     def residue(j, sums):
@@ -281,18 +314,23 @@
             t_s[j], picks(j), (((0,), (0,)), ((), ())), preferred_element_type=F32
         )
         x_s[j] = (keep * (mix_s[j].astype(F32) - wanted)).astype(BF16)
-        return take_chunk(j, sums, state)
-
-    sums = lax.fori_loop(0, nsp, residue, none)
+        return take_chunk(j, sums, q_t)
+
+    def next_residue(c, sums):
+        to_space(t_p.at[xor(nsp, me, c)], t_s.at[me], t_ss, t_rs, c).wait_recv()
+        return residue(xor(nsp, me, c), sums)
+
+    sums = lax.fori_loop(1, nsp, next_residue, residue(me, none))
     grad_states = send_states(1, sums)
-    take_states(1, grad_states)
+    take_states(1, grad_states, 0)
 
     def grad_copy(c):
         return to_space(grad_s.at[xor(nsp, me, c)], grad_o.at[part(me), :], g_ss, g_rs, c)
 
     def backward(i, carry):
         c = nsp - 1 - i
-        grad_s[xor(nsp, me, c)] = mix_chunk(xor(nsp, me, c), q_t, 0)
+        k = xor(nsp, me, c)
+        grad_s[k] = finish(k, dot_nt(xab[...], lines(k)), 0, 0)
 
         @pl.when(c > 0)
         def _():
@@ -324,6 +362,7 @@
     length = nsp * tok
     rows = inner // nsp
     unit = 0.065536 / (length * nsq)
+    fits = length * length <= 8 * 1024 * 1024
     hp = 16 * (-(-heads // 16))
     vmem = pl.BlockSpec(memory_space=pltpu.VMEM)
     dma = pltpu.SemaphoreType.DMA
@@ -339,12 +378,11 @@
             pltpu.VMEM((nsp, masked.shape[0], rows), BF16),
             pltpu.VMEM((nsp, masked.shape[0], rows), BF16),
             pltpu.VMEM((nsp, 2 * state + 16, tok), BF16),
-            pltpu.VMEM((rows, length), BF16),
-            pltpu.VMEM((rows, length), BF16),
+            pltpu.VMEM((2 * rows, length), BF16),
             pltpu.VMEM((nsp, rows, tok), BF16),
             pltpu.VMEM((nsp, rows, tok), BF16),
-            pltpu.VMEM((length, tok), BF16),
-            pltpu.VMEM((length, tok), BF16),
+            pltpu.VMEM((length, length if fits else tok), BF16),
+            pltpu.VMEM((16 if fits else tok, length), BF16),
             pltpu.VMEM((length, state), BF16),
             pltpu.VMEM((length, state), BF16),
             pltpu.VMEM((length, 128), F32),
@@ -356,8 +394,7 @@
             pltpu.VMEM((nsq, hp, 128), F32),
             pltpu.VMEM((2, 2, rows, state), F32),
             pltpu.VMEM((2, nsq, rows, state), F32),
-            pltpu.VMEM((2, rows, state), BF16),
-            pltpu.VMEM((2, rows, state), BF16),
+            pltpu.VMEM((2 * rows, 2 * state), BF16),
             *[dma((nsp,)) for _ in range(10)],
             dma((nsq,)), dma((nsq,)),
             dma((2, nsq)), dma((2, nsq)),

time: 116 us -> 122 us (1.052)
  Pallas kernels: 112 us -> 118 us
    pallas_call x1, Pallas kernels: 112 us -> 118 us  [per_device(): pl.pallas_call(partial(kernel, nsp, nsq, heads, unit), out_shape=(jax.Sha...]
where the time goes in v4:
time: 122 us
  Pallas kernels  118 us (97%)
  local copies, waits for them, and re-layouts  3.32 us (3%)
    pallas_call x1, Pallas kernels, per_device(): pl.pallas_call(partial(kernel, nsp, nsq, heads, unit), out_shape=(jax.Sha...  118 us
    unnamed x4, local copies, waits for them, and re-layouts  3.32 us

profile of v4, /device:TPU:0, one launch (start us, length us, event | category | flops | bytes accessed | tf_op | source)
XLA Modules:
  0.0 122.3 jit_solution(14339899032157886609)
XLA Ops:
  0.6 118.3 %shard_map.95 = (bf16[2048,256]{1,0:T(8,128)(2,1)}, bf16[2048,256]{1,0:T(8,128)(2,1)}) custom-call(bf16[2048,256]{1,0:T(8,128)(2,1)} %feat.1, bf16[2048,256]{1,0:T(8,128)(2,1)} %targ.1, bf16[128,256]{1,0:T(8,128)(2,1)} %write.1, bf16[128,256]{1,0:T(8,128)(2,1)} %read.1, s32[4,2048]{1,0:T(4,128)} %codes.1, s32[1,2048]{1,0:T(1,128)} %bitcast.2, ...), custom_call_target="tpu_custom_call" | custom-call | tf_op jit(solution)/shard_map/pallas_call | solution.py:369
  118.9 0.0 copy-start
  118.9 2.4 %copy.12 = bf16[2048,256]{1,0:T(8,128)(2,1)} copy(bf16[2048,256]{1,0:T(8,128)(2,1)} %get-tuple-element.4) | data formatting | bytes 2097152
  121.3 0.0 copy-done
  121.3 1.0 copy.13
Async XLA Ops:
  118.9 2.4 %copy-start = (bf16[2048,256]{1,0:T(8,128)(2,1)S(1)}, bf16[2048,256]{1,0:T(8,128)(2,1)}, u32[]{:S(2)}) copy-start(bf16[2048,256]{1,0:T(8,128)(2,1)} %get-tuple-element.5) | copy-start | bytes 3145732

commit v5 on v4

--- a/solution.py
+++ b/solution.py
@@ -165,6 +165,13 @@
     while m > 1:
         m //= 2
         key_step(m)
+    t_copies = {
+        c: to_space(t_p.at[xor(nsp, me, c)], t_s.at[me], t_ss, t_rs, c) for c in range(1, nsp)
+    }
+    for c in reversed(range(1, nsp)):
+        x_copies[c].wait_send()
+        t_copies[c].start()
+    t_s[me] = t_p[me]
     for c in range(1, nsp, 2):
         key_copies[c].wait_recv()
 
@@ -208,17 +215,6 @@
 
         lax.fori_loop(0, nsp, fill, 0)
         return gm_r[...]
-
-    if whole:
-
-        def fill_all(j, carry):
-            def fill(k, carry):
-                gm_c[chunk(j), chunk(k)] = gram(j, k)
-                return carry
-
-            return lax.fori_loop(0, nsp, fill, carry)
-
-        lax.fori_loop(0, nsp, fill_all, 0)
 
     def take_chunk(j, sums, into_t):
         value = x_s[j].astype(F32)
@@ -279,16 +275,19 @@
         return take_chunk(xor(nsp, me, c), sums, w_t)
 
     sums = take_chunk(me, none, w_t)
-    sums = lax.fori_loop(1, nsp // 2, x_chunk, sums)
-    t_copies = {
-        c: to_space(t_p.at[xor(nsp, me, c)], t_s.at[me], t_ss, t_rs, c) for c in range(1, nsp)
-    }
-    for c in reversed(range(1, nsp)):
-        x_copies[c].wait_send()
-        t_copies[c].start()
-    t_s[me] = t_p[me]
-    sums = lax.fori_loop(nsp // 2, nsp, x_chunk, sums)
+    sums = lax.fori_loop(1, nsp, x_chunk, sums)
     states = send_states(0, sums)
+    if whole:
+
+        def fill_all(j, carry):
+            def fill(k, carry):
+                gm_c[chunk(j), chunk(k)] = gram(j, k)
+                return carry
+
+            return lax.fori_loop(0, nsp, fill, carry)
+
+        lax.fori_loop(0, nsp, fill_all, 0)
+
     take_states(0, states, 1)
 
     def mixed_copy(c):

time: 122 us -> 110 us (0.902)
  Pallas kernels: 118 us -> 106 us
    pallas_call x1, Pallas kernels: 118 us -> 106 us  [per_device(): pl.pallas_call(partial(kernel, nsp, nsq, heads, unit), out_shape=(jax.Sha...]
where the time goes in v5:
time: 110 us
  Pallas kernels  106 us (96%)
  local copies, waits for them, and re-layouts  3.32 us (3%)
    pallas_call x1, Pallas kernels, per_device(): pl.pallas_call(partial(kernel, nsp, nsq, heads, unit), out_shape=(jax.Sha...  106 us
    unnamed x4, local copies, waits for them, and re-layouts  3.32 us

profile of v5, /device:TPU:0, one launch (start us, length us, event | category | flops | bytes accessed | tf_op | source)
XLA Modules:
  0.0 110.1 jit_solution(17640300738136420936)
XLA Ops:
  0.6 106.1 %shard_map.95 = (bf16[2048,256]{1,0:T(8,128)(2,1)}, bf16[2048,256]{1,0:T(8,128)(2,1)}) custom-call(bf16[2048,256]{1,0:T(8,128)(2,1)} %feat.1, bf16[2048,256]{1,0:T(8,128)(2,1)} %targ.1, bf16[128,256]{1,0:T(8,128)(2,1)} %write.1, bf16[128,256]{1,0:T(8,128)(2,1)} %read.1, s32[4,2048]{1,0:T(4,128)} %codes.1, s32[1,2048]{1,0:T(1,128)} %bitcast.2, ...), custom_call_target="tpu_custom_call" | custom-call | tf_op jit(solution)/shard_map/pallas_call | solution.py:368
  106.7 0.0 copy-start
  106.7 2.4 %copy.12 = bf16[2048,256]{1,0:T(8,128)(2,1)} copy(bf16[2048,256]{1,0:T(8,128)(2,1)} %get-tuple-element.4) | data formatting | bytes 2097152
  109.1 0.0 copy-done
  109.1 1.0 copy.13
Async XLA Ops:
  106.7 2.4 %copy-start = (bf16[2048,256]{1,0:T(8,128)(2,1)S(1)}, bf16[2048,256]{1,0:T(8,128)(2,1)}, u32[]{:S(2)}) copy-start(bf16[2048,256]{1,0:T(8,128)(2,1)} %get-tuple-element.5) | copy-start | bytes 3145732

commit v6 on v5

--- a/solution.py
+++ b/solution.py
@@ -35,7 +35,7 @@
     mixed_o, grad_o,
     x_s, t_s, t_p, slab, xab, mix_s, grad_s, gm_c, gm_r, w_t, q_t, rank_c, rank_r, codes_f, a_s, b_s,
     tot_s, tot_r, st_s, st_r, sab,
-    key_ss, key_rs, x_ss, x_rs, t_ss, t_rs, m_ss, m_rs, g_ss, g_rs, tot_ss, tot_rs, st_ss, st_rs,
+    key_ss, key_rs, x_ss, x_rs, t_ss, t_rs, m_ss, m_rs, g_ss, g_rs, tot_ss, tot_rs, st_ss, st_rs, own_ss, targ_s,
 ):
     me, mine = lax.axis_index("space"), lax.axis_index("seq")
     tok = feat.shape[1]
@@ -95,6 +95,8 @@
             key_copies[m + c] = key_copy(m, c)
             key_copies[m + c].start()
 
+    own_t = pltpu.make_async_copy(targ, targ_s, own_ss.at[1])
+    own_t.start()
     key_step(nsp // 2)
     tot_copies = [to_seq(tot_s, tot_r.at[c], tot_ss, tot_rs, c) for c in range(1, nsq)]
     for copy in tot_copies:
@@ -104,7 +106,8 @@
     }
     for c in range(1, nsp // 2):
         x_copies[c].start()
-    x_s[me] = feat[part(me), :]
+    own_x = pltpu.make_async_copy(feat.at[part(me), :], x_s.at[me], own_ss.at[0])
+    own_x.start()
 
     length = nsp * tok
     places = lax.broadcasted_iota(jnp.int32, (tok, length), 1).astype(F32)
@@ -137,11 +140,16 @@
     for c in reversed(range(nsp // 2, nsp)):
         x_copies[c].start()
 
+    own_t.wait()
+
     def pack(d, carry):
-        t_p[d] = dot_nt(picks(me), targ[part(d), :]).astype(BF16)
+        t_p[d] = dot_nt(picks(me), targ_s[part(d), :]).astype(BF16)
         return carry
 
     lax.fori_loop(0, nsp, pack, 0)
+    while m > 1:
+        m //= 2
+        key_step(m)
 
     for copy in tot_copies:
         copy.wait_recv()
@@ -162,9 +170,6 @@
 
     lax.fori_loop(0, nsp, run_chunk, 0)
 
-    while m > 1:
-        m //= 2
-        key_step(m)
     t_copies = {
         c: to_space(t_p.at[xor(nsp, me, c)], t_s.at[me], t_ss, t_rs, c) for c in range(1, nsp)
     }
@@ -274,6 +279,7 @@
         to_space(feat.at[part(xor(nsp, me, c)), :], x_s.at[me], x_ss, x_rs, c).wait_recv()
         return take_chunk(xor(nsp, me, c), sums, w_t)
 
+    own_x.wait()
     sums = take_chunk(me, none, w_t)
     sums = lax.fori_loop(1, nsp, x_chunk, sums)
     states = send_states(0, sums)
@@ -305,7 +311,8 @@
         return carry
 
     lax.fori_loop(0, nsp, forward, 0)
-    mixed_o[part(me), :] = mix_s[me]
+    own_m = pltpu.make_async_copy(mix_s.at[me], mixed_o.at[part(me), :], own_ss.at[2])
+    own_m.start()
 
     def residue(j, sums):
         keep = slab[j, 2 * state : 2 * state + 16, :].astype(F32)[0:1, :]
@@ -338,7 +345,8 @@
         return carry
 
     lax.fori_loop(0, nsp, backward, 0)
-    grad_o[part(me), :] = grad_s[me]
+    own_g = pltpu.make_async_copy(grad_s.at[me], grad_o.at[part(me), :], own_ss.at[3])
+    own_g.start()
 
     for c in range(1, nsp):
         key_copies[c].wait_send()
@@ -349,6 +357,8 @@
     for c in range(1, nsp):
         mixed_copy(c).wait()
         grad_copy(c).wait()
+    own_m.wait()
+    own_g.wait()
 
 
 def per_device(
@@ -364,14 +374,15 @@
     fits = length * length <= 8 * 1024 * 1024
     hp = 16 * (-(-heads // 16))
     vmem = pl.BlockSpec(memory_space=pltpu.VMEM)
+    hbm = pl.BlockSpec(memory_space=pl.ANY)
     dma = pltpu.SemaphoreType.DMA
     return pl.pallas_call(
         partial(kernel, nsp, nsq, heads, unit),
         out_shape=(
             jax.ShapeDtypeStruct((inner, tok), BF16), jax.ShapeDtypeStruct((inner, tok), BF16)
         ),
-        in_specs=[vmem] * 7 + [pl.BlockSpec(memory_space=pltpu.SMEM)],
-        out_specs=(vmem, vmem),
+        in_specs=[hbm] * 2 + [vmem] * 5 + [pl.BlockSpec(memory_space=pltpu.SMEM)],
+        out_specs=(hbm, hbm),
         scratch_shapes=[
             pltpu.VMEM((nsp, rows, tok), BF16),
             pltpu.VMEM((nsp, masked.shape[0], rows), BF16),
@@ -396,7 +407,8 @@
             pltpu.VMEM((2 * rows, 2 * state), BF16),
             *[dma((nsp,)) for _ in range(10)],
             dma((nsq,)), dma((nsq,)),
-            dma((2, nsq)), dma((2, nsq)),
+            dma((2, nsq)), dma((2, nsq)), dma((4,)),
+            pltpu.VMEM((inner, tok), BF16),
         ],
         compiler_params=pltpu.CompilerParams(
             collective_id=0, has_side_effects=True, vmem_limit_bytes=56 * 1024 * 1024

time: 110 us -> 109 us (level)
    pallas_call x1, Pallas kernels: 106 us -> 105 us  [per_device(): pl.pallas_call(partial(kernel, nsp, nsq, heads, unit), out_shape=(jax.Sha...]
where the time goes in v6:
time: 109 us
  Pallas kernels  105 us (96%)
  local copies, waits for them, and re-layouts  3.32 us (3%)
    pallas_call x1, Pallas kernels, per_device(): pl.pallas_call(partial(kernel, nsp, nsq, heads, unit), out_shape=(jax.Sha...  105 us
    unnamed x4, local copies, waits for them, and re-layouts  3.32 us

profile of v6, /device:TPU:0, one launch (start us, length us, event | category | flops | bytes accessed | tf_op | source)
XLA Modules:
  0.0 108.9 jit_solution(10043680957352946081)
XLA Ops:
  0.6 104.9 %shard_map.95 = (bf16[2048,256]{1,0:T(8,128)(2,1)}, bf16[2048,256]{1,0:T(8,128)(2,1)}) custom-call(bf16[2048,256]{1,0:T(8,128)(2,1)} %feat.1, bf16[2048,256]{1,0:T(8,128)(2,1)} %targ.1, bf16[128,256]{1,0:T(8,128)(2,1)} %write.1, bf16[128,256]{1,0:T(8,128)(2,1)} %read.1, s32[4,2048]{1,0:T(4,128)} %codes.1, s32[1,2048]{1,0:T(1,128)} %bitcast.2, ...), custom_call_target="tpu_custom_call" | custom-call | tf_op jit(solution)/shard_map/pallas_call | solution.py:379
  105.6 0.0 copy-start
  105.6 2.4 %copy.12 = bf16[2048,256]{1,0:T(8,128)(2,1)} copy(bf16[2048,256]{1,0:T(8,128)(2,1)} %get-tuple-element.4) | data formatting | bytes 2097152
  107.9 0.0 copy-done
  107.9 1.0 copy.13
Async XLA Ops:
  105.6 2.4 %copy-start = (bf16[2048,256]{1,0:T(8,128)(2,1)S(1)}, bf16[2048,256]{1,0:T(8,128)(2,1)}, u32[]{:S(2)}) copy-start(bf16[2048,256]{1,0:T(8,128)(2,1)} %get-tuple-element.5) | copy-start | bytes 3145732

commit v7 on v6

--- a/solution.py
+++ b/solution.py
@@ -104,7 +104,7 @@
     x_copies = {
         c: to_space(feat.at[part(xor(nsp, me, c)), :], x_s.at[me], x_ss, x_rs, c) for c in range(1, nsp)
     }
-    for c in range(1, nsp // 2):
+    for c in (nsp - 1, *range(1, nsp // 2)):
         x_copies[c].start()
     own_x = pltpu.make_async_copy(feat.at[part(me), :], x_s.at[me], own_ss.at[0])
     own_x.start()
@@ -137,7 +137,7 @@
 
     m = nsp // 4
     key_step(m)
-    for c in reversed(range(nsp // 2, nsp)):
+    for c in reversed(range(nsp // 2, nsp - 1)):
         x_copies[c].start()
 
     own_t.wait()

time: 109 us -> 112 us (1.028)
  Pallas kernels: 105 us -> 108 us
    pallas_call x1, Pallas kernels: 105 us -> 108 us  [per_device(): pl.pallas_call(partial(kernel, nsp, nsq, heads, unit), out_shape=(jax.Sha...]
where the time goes in v7:
time: 112 us
  Pallas kernels  108 us (96%)
  local copies, waits for them, and re-layouts  3.32 us (3%)
    pallas_call x1, Pallas kernels, per_device(): pl.pallas_call(partial(kernel, nsp, nsq, heads, unit), out_shape=(jax.Sha...  108 us
    unnamed x4, local copies, waits for them, and re-layouts  3.32 us

profile of v7, /device:TPU:0, one launch (start us, length us, event | category | flops | bytes accessed | tf_op | source)
XLA Modules:
  0.0 111.8 jit_solution(557274795679517638)
XLA Ops:
  0.6 107.8 %shard_map.95 = (bf16[2048,256]{1,0:T(8,128)(2,1)}, bf16[2048,256]{1,0:T(8,128)(2,1)}) custom-call(bf16[2048,256]{1,0:T(8,128)(2,1)} %feat.1, bf16[2048,256]{1,0:T(8,128)(2,1)} %targ.1, bf16[128,256]{1,0:T(8,128)(2,1)} %write.1, bf16[128,256]{1,0:T(8,128)(2,1)} %read.1, s32[4,2048]{1,0:T(4,128)} %codes.1, s32[1,2048]{1,0:T(1,128)} %bitcast.2, ...), custom_call_target="tpu_custom_call" | custom-call | tf_op jit(solution)/shard_map/pallas_call | solution.py:379
  108.4 0.0 copy-start
  108.4 2.4 %copy.12 = bf16[2048,256]{1,0:T(8,128)(2,1)} copy(bf16[2048,256]{1,0:T(8,128)(2,1)} %get-tuple-element.4) | data formatting | bytes 2097152
  110.8 0.0 copy-done
  110.8 1.0 copy.13
Async XLA Ops:
  108.4 2.4 %copy-start = (bf16[2048,256]{1,0:T(8,128)(2,1)S(1)}, bf16[2048,256]{1,0:T(8,128)(2,1)}, u32[]{:S(2)}) copy-start(bf16[2048,256]{1,0:T(8,128)(2,1)} %get-tuple-element.5) | copy-start | bytes 3145732
